TPU v7x, 32 devices: a whole 2x2x4 slice. The times are simulated.
32 devices in a mesh: dp: 8 (over z, x), mp: 4 (over y, core).
Axes of the slice: x: 2, y: 2, z: 4, core: 2. Of those that a mesh axis runs over, the one named last changes fastest.
Arguments:
- states: bfloat16 [65536, 2048], P(('dp', 'mp')), may hold values from -6 to 6
- dest_device: int32 [65536, 1], P(('dp', 'mp')), may hold values from 0 to 7; in each aligned block of 2048 rows (0 to 2047, 2048 to 4095, ...) at most 320 rows name the same one
- goals: bfloat16 [81920, 1024], P(('dp', 'mp')), may hold values from -6 to 6
- returns: bfloat16 [81920], P(('dp', 'mp')), may hold values from -9 to 9
- weight_in: bfloat16 [3072, 512], P('mp'), may hold values from -0.109375 to 0.109375
- weight_hidden: bfloat16 [3, 512, 512], P(None, 'mp'), may hold values from -0.25 to 0.25
- norm_gain: bfloat16 [4, 512], P(None, 'mp'), may hold values from 0.5 to 1.5
- norm_shift: bfloat16 [4, 512], P(None, 'mp'), may hold values from -1.5 to 1.5
- weight_out: bfloat16 [512], P('mp'), may hold values from -0.25 to 0.25
Outputs:
- total_loss: float32 [], replicated
- grad_states: bfloat16 [65536, 2048], P(('dp', 'mp'))
- grad_goals: bfloat16 [81920, 1024], P(('dp', 'mp'))
- grad_weight_in: float32 [3072, 512], P(None, ('dp', 'mp'))
- grad_weight_hidden: float32 [3, 512, 512], P(None, None, ('dp', 'mp'))
- grad_norm_gain: float32 [4, 512], P(None, ('dp', 'mp'))
- grad_norm_shift: float32 [4, 512], P(None, ('dp', 'mp'))
- grad_weight_out: float32 [512], P(('dp', 'mp'))
Inputs may be any that keep to these rules, and one draw needn't show every extreme that they name: `dest_device`: the 2048 rows of one device name each destination at most 320 times, a bound that some block reaches.
All inputs are finite; a program needn't handle non-finite values.
Results may differ from a plain program's by a relative error of at most 0.019.
Values may be sent and summed in bfloat16 or wider, within the bound.
No kernel may reach another device: no remote copies, remote signals or barrier semaphores. Data moves between devices by JAX's collectives and lax.ppermute only.
A program may use at most 192 MiB of HBM per device.

v0:
```python
import jax
import jax.numpy as jnp
from jax import lax
from jax.sharding import PartitionSpec as P


def norm_act(values, gain, shift):
    center = values - jnp.mean(values, axis=-1, keepdims=True)
    spread = jnp.mean(center * center, axis=-1, keepdims=True)
    return jax.nn.elu(center * lax.rsqrt(spread + 1e-05) * gain + shift)


def left_product(first, second):
    return lax.dot_general(
        first, second, (((0,), (0,)), ((), ())), preferred_element_type=jnp.float32
    )


def right_product(first, second):
    return lax.dot_general(
        first, second, (((1,), (1,)), ((), ())), preferred_element_type=jnp.float32
    )


def shards(
    states, dest_device, goals, returns, weight_in, weight_hidden, norm_gain, norm_shift, weight_out
):
    dp_count = lax.axis_size("dp")
    all_rows = states.shape[0] * dp_count * lax.axis_size("mp")
    slot_count = returns.shape[0]
    capacity = slot_count // dp_count
    feat_width = states.shape[1]
    layer_count = norm_gain.shape[0]
    full_in, full_hidden, full_gain, full_shift, full_out = (
        lax.all_gather(weight_in, "mp", axis=0, tiled=True),
        lax.all_gather(weight_hidden, "mp", axis=1, tiled=True),
        lax.all_gather(norm_gain, "mp", axis=1, tiled=True),
        lax.all_gather(norm_shift, "mp", axis=1, tiled=True),
        lax.all_gather(weight_out, "mp", axis=0, tiled=True),
    )
    dest_index = dest_device[:, 0]
    dest_onehot = (dest_index[:, None] == jnp.arange(dp_count, dtype=jnp.int32)[None, :]).astype(
        jnp.int32
    )
    rank_within = jnp.sum((jnp.cumsum(dest_onehot, axis=0) - dest_onehot) * dest_onehot, axis=1)
    slot_index = dest_index * capacity + rank_within
    send_states = jnp.zeros((slot_count, feat_width), jnp.bfloat16).at[slot_index].set(states)
    send_marks = (
        jnp.zeros((slot_count,), jnp.bfloat16)
        .at[slot_index]
        .set(jnp.ones_like(dest_index, jnp.bfloat16))
    )
    got_states, got_marks = (
        lax.all_to_all(
            send_states.reshape(dp_count, capacity, feat_width),
            "dp",
            split_axis=0,
            concat_axis=0,
            tiled=True,
        ),
        lax.all_to_all(
            send_marks.reshape(dp_count, capacity), "dp", split_axis=0, concat_axis=0, tiled=True
        ),
    )
    row_states = got_states.reshape(slot_count, feat_width)
    valid_mask = got_marks.reshape(slot_count).astype(jnp.float32)
    return_values = returns.astype(jnp.float32)
    local_square = jnp.sum(valid_mask * return_values * return_values)
    square_total = lax.psum(local_square, ("dp", "mp"))
    scale_value = jnp.sqrt(square_total / all_rows + 1e-06)
    inputs = jnp.concatenate([row_states, goals], axis=1)
    layer_inputs = [inputs]
    pullbacks = []
    hidden = inputs
    for layer_number in range(layer_count):
        matrix = full_in if layer_number == 0 else full_hidden[layer_number - 1]
        projected = jnp.dot(hidden, matrix, preferred_element_type=jnp.float32)
        activated, pullback = jax.vjp(
            norm_act,
            projected,
            full_gain[layer_number].astype(jnp.float32),
            full_shift[layer_number].astype(jnp.float32),
        )
        hidden = activated.astype(jnp.bfloat16)
        pullbacks.append(pullback)
        layer_inputs.append(hidden)
    value_pred = jnp.dot(hidden, full_out, preferred_element_type=jnp.float32)
    row_error = valid_mask * (value_pred - return_values / scale_value)
    total_loss = lax.psum(0.5 * jnp.sum(row_error * row_error) / all_rows, ("dp", "mp"))
    grad_value = (row_error / all_rows).astype(jnp.bfloat16)
    grad_out = jnp.dot(grad_value, hidden, preferred_element_type=jnp.float32)
    grad_hidden = grad_value.astype(jnp.float32)[:, None] * full_out.astype(jnp.float32)[None, :]
    hidden_grads = [None] * (layer_count - 1)
    gain_grads = [None] * layer_count
    shift_grads = [None] * layer_count
    grad_in = None
    for layer_number in reversed(range(layer_count)):
        grad_pre, grad_gain, grad_shift = pullbacks[layer_number](grad_hidden)
        grad_pre = grad_pre.astype(jnp.bfloat16)
        gain_grads[layer_number] = grad_gain
        shift_grads[layer_number] = grad_shift
        matrix = full_in if layer_number == 0 else full_hidden[layer_number - 1]
        weight_grad = left_product(layer_inputs[layer_number], grad_pre)
        if layer_number > 0:
            hidden_grads[layer_number - 1] = weight_grad
        else:
            grad_in = weight_grad
        grad_hidden = right_product(grad_pre, matrix)
    grad_state_rows = grad_hidden[:, :feat_width].astype(jnp.bfloat16)
    grad_goal_rows = grad_hidden[:, feat_width:].astype(jnp.bfloat16)
    came_back = lax.all_to_all(
        grad_state_rows.reshape(dp_count, capacity, feat_width),
        "dp",
        split_axis=0,
        concat_axis=0,
        tiled=True,
    )
    grad_states = came_back.reshape(slot_count, feat_width)[slot_index]
    shares = (
        lax.psum_scatter(grad_in, ("dp", "mp"), scatter_dimension=1, tiled=True),
        lax.psum_scatter(jnp.stack(hidden_grads), ("dp", "mp"), scatter_dimension=2, tiled=True),
        lax.psum_scatter(jnp.stack(gain_grads), ("dp", "mp"), scatter_dimension=1, tiled=True),
        lax.psum_scatter(jnp.stack(shift_grads), ("dp", "mp"), scatter_dimension=1, tiled=True),
        lax.psum_scatter(grad_out, ("dp", "mp"), scatter_dimension=0, tiled=True),
    )
    return (
        total_loss,
        grad_states,
        grad_goal_rows,
        shares[0],
        shares[1],
        shares[2],
        shares[3],
        shares[4],
    )


def solution(mesh):
    placed = (
        P(("dp", "mp"), None),
        P(("dp", "mp"), None),
        P(("dp", "mp"), None),
        P(("dp", "mp")),
        P("mp", None),
        P(None, "mp", None),
        P(None, "mp"),
        P(None, "mp"),
        P("mp"),
    )
    return jax.shard_map(
        shards,
        mesh=mesh,
        in_specs=placed,
        out_specs=(
            P(),
            P(("dp", "mp"), None),
            P(("dp", "mp"), None),
            P(None, ("dp", "mp")),
            P(None, None, ("dp", "mp")),
            P(None, ("dp", "mp")),
            P(None, ("dp", "mp")),
            P(("dp", "mp")),
        ),
        check_vma=False,
    )
```

profile of v0, /device:TPU:0, one launch (start us, length us, event | category | flops | bytes accessed | tf_op | source)
XLA Modules:
  0.0 1056.6 jit_solution(1476735436434677186)
XLA Ops:
  12.2 14.6 %scatter_custom_fusion = bf16[2560]{0:T(1024)(128)(2,1)S(1)} fusion(s32[2048]{0:T(1024)S(1)} %bitcast.104, bf16[2048]{0:T(1024)(128)(2,1)S(1)} %broadcast.175, bf16[]{:T(256)} %constant.61.clone.1), kind=kCustom, calls=%fused_computation.111 | custom fusion | bytes 5122 | tf_op jit(solution)/shard_map/scatter | solution.py:51
  28.7 7.3 all-to-all-start
  36.0 19.2 %scatter_custom_fusion.1 = bf16[2560,2048]{1,0:T(8,128)(2,1)} fusion(s32[2048]{0:T(1024)S(1)} %bitcast.105, bf16[2048,2048]{1,0:T(8,128)(2,1)} %param.9, bf16[]{:T(256)} %constant.61.clone.1), kind=kCustom, calls=%fused_computation.54 | custom fusion | bytes 10486272 | tf_op jit(solution)/shard_map/scatter | solution.py:47
  55.3 6.1 all-to-all-start.1
  62.9 5.0 all-gather
  68.0 5.1 all_gather.16
  73.0 5.1 all_gather.17
  78.9 230.2 %psum.14 = f32[]{:T(128)} all-reduce(f32[]{:T(128)} %fusion.26), channel_id=1, replica_groups=mesh['dp'=8,'mp'=4] {'dp','mp'}, use_global_device_ids=true, to_apply=%region_14.15 | all-reduce | flops 1 | bytes 8 | tf_op jit(solution)/shard_map/psum | solution.py:69
  309.9 14.7 %fusion.48 = (f32[2560]{0:T(1024)S(1)}, f32[2560,512]{0,1:T(8,128)}) fusion(bf16[3072,512]{1,0:T(8,128)(2,1)} %all-gather.4.cloned.1.call-done, bf16[2560,1024]{1,0:T(8,128)(2,1)} %param.11, bf16[2560,2048]{1,0:T(8,128)(2,1)} %bitcast.6), kind=kOutput, calls=%fused_computation.132 | convolution fusion | flops 8085829120 | bytes 24127488 | tf_op jit(solution)/shard_map/dot_general | solution.py:77
  327.7 6.2 fusion.49
  336.5 3.7 fusion.50
  340.8 3.9 fusion.51
  349.4 4.6 fusion.42
  354.0 4.0 fusion.46
  358.0 6.5 multiply_reduce_fusion.1
  364.6 6.5 fusion.45
  371.1 8.6 multiply_reduce_fusion.2
  379.7 4.0 fusion.44
  383.7 4.3 multiply_reduce_fusion.3
  391.9 13.9 %convolution_convert_fusion = bf16[2560,3072]{1,0:T(8,128)(2,1)} fusion(bf16[3072,512]{1,0:T(8,128)(2,1)} %all-gather.4.cloned.1.call-done, f32[2560,512]{0,1:T(8,128)S(1)} %get-tuple-element.47, f32[2560]{0:T(1024)S(1)} %negate_multiply_fusion), kind=kOutput, calls=%fused_computation.3 | convolution fusion | flops 8063549440 | bytes 24127488 | tf_op jit(solution)/shard_map/dot_general | solution.py:20
  405.8 10.2 slice.79
  415.9 5.3 all-to-all-start.2
  423.2 7.3 convolution_bitcast_fusion
  430.5 7.3 convolution_bitcast_fusion.1
  443.0 5.1 copy.38
  448.4 15.0 %fusion = f32[3072,512]{0,1:T(8,128)} fusion(bf16[2560,1024]{1,0:T(8,128)(2,1)} %param.11, bf16[2560,2048]{1,0:T(8,128)(2,1)} %bitcast.6, f32[2560,512]{0,1:T(8,128)} %copy-done.2, f32[2560]{0:T(1024)S(1)} %negate_multiply_fusion), kind=kOutput, calls=%fused_computation.5 | convolution fusion | flops 8087142400 | bytes 27273216 | tf_op jit(solution)/shard_map/dot_general | solution.py:14
  465.5 205.4 %all-reduce.2 = (f32[]{:T(128)}, f32[512]{0:T(512)S(1)}) all-reduce(f32[]{:T(128)S(6)} %div.101, f32[512]{0:T(512)S(1)} %bitcast.116), channel_id=1, replica_groups=mesh['dp'=8,'mp'=4] {'dp','mp'}, use_global_device_ids=true, to_apply=%region_16.17 | all-reduce | flops 513 | bytes 4104 | tf_op jit(solution)/shard_map/psum | solution.py:89
  671.0 5.4 slice.80
  678.4 108.2 %reduce-scatter.10.cloned.1.call-done = f32[16,4]{1,0:T(8,128)} async-done(((f32[512,4]{1,0:T(8,128)}), f32[16,4]{1,0:T(8,128)}) %reduce-scatter.10.cloned.1.call-update) | async-done | bytes 272
  787.9 142.3 %all-reduce.5.cloned.1.call-done = f32[3,512,512]{1,0,2:T(4,128)} async-done(((f32[3,512,512]{1,0,2:T(4,128)}), f32[3,512,512]{1,0,2:T(4,128)}) %all-reduce.5.cloned.1.call-update) | async-done | bytes 3145744
  931.8 21.6 %gather_fusion = bf16[2048,2048]{1,0:T(8,128)(2,1)} fusion(bf16[2560,2048]{1,0:T(8,128)(2,1)} %bitcast.20, s32[2048]{0:T(1024)S(1)} %broadcast_clamp_fusion), kind=kCustom, calls=%fused_computation | custom fusion | bytes 16785408 | tf_op jit(solution)/shard_map/gather | solution.py:118
  953.5 96.1 %reduce-scatter.8.cloned.1.call-done = f32[3072,16]{0,1:T(8,128)} async-done(((f32[3072,512]{0,1:T(8,128)}), f32[3072,16]{0,1:T(8,128)}) %reduce-scatter.8.cloned.1.call-update) | async-done | bytes 196624 | tf_op jit(solution)/shard_map/reduce_scatter | solution.py:120
  (115 shorter events, 37.9 us)
Async XLA Ops:
  12.2 43.0 %copy-start.5 = (s32[2048,1]{0,1:T(1,128)}, s32[2048,1]{0,1:T(1,128)S(1)}, u32[]{:S(2)}) copy-start(s32[2048,1]{0,1:T(1,128)S(1)} %compare_select_fusion.8) | copy-start | bytes 24580
  28.7 26.5 %all-to-all-start = ((bf16[8,2,160]{2,1,0:T(2,128)(2,1)}), bf16[8,2,160]{2,1,0:T(2,128)(2,1)S(1)}, u32[]{:S(2)}, u32[]{:S(2)}) async-start(bf16[8,2,160]{2,1,0:T(2,128)(2,1)} %reshape.256), calls=%async_computation | async-start | bytes 16384 | tf_op jit(solution)/shard_map/all_to_all | solution.py:61
  55.2 7.7 copy-start.10
  55.2 12.7 %copy-start.8 = (bf16[4,128]{1,0:T(4,128)(2,1)S(1)}, bf16[4,128]{1,0:T(4,128)(2,1)}, u32[]{:S(2)}) copy-start(bf16[4,128]{1,0:T(4,128)(2,1)} %param.15) | copy-start | bytes 3076
  55.2 17.8 %copy-start.9 = (bf16[4,128]{1,0:T(4,128)(2,1)S(1)}, bf16[4,128]{1,0:T(4,128)(2,1)}, u32[]{:S(2)}) copy-start(bf16[4,128]{1,0:T(4,128)(2,1)} %param.16) | copy-start | bytes 3076
  55.2 23.1 %copy-start.7 = (bf16[2560]{0:T(1024)(128)(2,1)S(1)}, bf16[2560]{0:T(1024)(128)(2,1)}, u32[]{:S(2)}) copy-start(bf16[2560]{0:T(1024)(128)(2,1)} %param.12) | copy-start | bytes 15364
  55.3 254.6 %all-to-all-start.1 = ((bf16[8,320,2048]{2,1,0:T(8,128)(2,1)}), bf16[8,320,2048]{2,1,0:T(8,128)(2,1)}, u32[]{:S(2)}, u32[]{:S(2)}) async-start(bf16[8,320,2048]{2,1,0:T(8,128)(2,1)} %bitcast.92), calls=%async_computation.1 | async-start | bytes 20971520 | tf_op jit(solution)/shard_map/all_to_all | solution.py:54
  61.4 248.5 %all-gather.4.cloned.1.call-start = ((), (), s32[]{:S(2)}) async-start(), calls=%async_computation.6 | async-start | bytes 3932160 | tf_op jit(solution)/shard_map/all_gather | solution.py:35
  62.1 265.5 %all-gather.6.cloned.1.call-start = ((), (), s32[]{:S(2)}) async-start(), calls=%async_computation.7 | async-start | bytes 1966080 | tf_op jit(solution)/shard_map/all_gather | solution.py:36
  333.9 45.8 %copy-start = (f32[2560,512]{0,1:T(8,128)}, f32[2560,512]{0,1:T(8,128)S(1)}, u32[]{:S(2)}) copy-start(f32[2560,512]{0,1:T(8,128)S(1)} %get-tuple-element.68) | copy-start | bytes 15728644
  333.9 2.6 copy-start.11
  340.2 24.4 %copy-start.1 = (f32[2560,512]{0,1:T(8,128)}, f32[2560,512]{0,1:T(8,128)S(1)}, u32[]{:S(2)}) copy-start(f32[2560,512]{0,1:T(8,128)S(1)} %get-tuple-element.70) | copy-start | bytes 15728644
  358.0 6.5 copy-start.4
  364.6 19.1 %slice-start = ((s8[5242880]{0:T(1024)(128)(4,1)}), s8[4194304]{0:T(1024)(128)(4,1)S(1)}, s32[]{:S(2)}) async-start(s8[5242880]{0:T(1024)(128)(4,1)} %bitcast.93), calls=%async_computation.12 | async-start | bytes 8388608
  371.1 12.6 %slice-start.1 = ((s8[5242880]{0:T(1024)(128)(4,1)}), s8[1048576]{0:T(1024)(128)(4,1)S(1)}, s32[]{:S(2)}) async-start(s8[5242880]{0:T(1024)(128)(4,1)} %bitcast.93), calls=%async_computation.13 | async-start | bytes 2097152
  383.7 4.4 copy-start.3
  389.6 2.3 copy-start.2
  415.9 515.9 %all-to-all-start.2 = ((bf16[8,320,2048]{2,1,0:T(8,128)(2,1)}), bf16[8,320,2048]{2,1,0:T(8,128)(2,1)}, u32[]{:S(2)}, u32[]{:S(2)}) async-start(bf16[8,320,2048]{2,1,0:T(8,128)(2,1)} %bitcast.91), calls=%async_computation.2 | async-start | bytes 20971520 | tf_op jit(solution)/shard_map/all_to_all | solution.py:111
  421.2 255.8 %reduce-scatter.12.cloned.1.call-start = ((), (), s32[]{:S(2)}) async-start(), calls=%async_computation.10 | async-start | bytes 270336
  422.2 364.4 %reduce-scatter.10.cloned.1.call-start = ((), (), s32[]{:S(2)}) async-start(), calls=%async_computation.9 | async-start | bytes 270336
  423.2 507.0 %all-reduce.5.cloned.1.call-start = ((), (), s32[]{:S(2)}) async-start(), calls=%async_computation.11 | async-start | bytes 8388608
  423.2 14.6 %slice-start.2 = ((s8[5242880]{0:T(1024)(128)(4,1)}), s8[4194304]{0:T(1024)(128)(4,1)S(1)}, s32[]{:S(2)}) async-start(s8[5242880]{0:T(1024)(128)(4,1)} %bitcast.95), calls=%async_computation.14 | async-start | bytes 8388608
  423.2 14.6 %slice-start.4 = ((s8[5242880]{0:T(1024)(128)(4,1)}), s8[4194304]{0:T(1024)(128)(4,1)S(1)}, s32[]{:S(2)}) async-start(s8[5242880]{0:T(1024)(128)(4,1)} %bitcast.97), calls=%async_computation.16 | async-start | bytes 8388608
  430.5 7.3 slice-start.3
  430.5 7.3 slice-start.5
  448.1 601.4 %reduce-scatter.8.cloned.1.call-start = ((), (), s32[]{:S(2)}) async-start(), calls=%async_computation.8 | async-start | bytes 6488064 | tf_op jit(solution)/shard_map/reduce_scatter | solution.py:120
  463.4 0.7 copy-start.6
Sparse Core Ops, SparseCore 0:
  63.8 30.3 all-gather.3
  95.7 19.6 all-gather.5
  424.3 225.9 reduce-scatter.11
  652.4 134.1 reduce-scatter.9
  792.5 137.6 all-reduce.4
  936.3 113.2 reduce-scatter.7
where the time goes:
time: 1060 us
  blocking collectives  451 us (43%)
  waiting for transfers between devices  348 us (33%)
  matrix products  95.7 us (9%)
  local copies, waits for them, and re-layouts  89.4 us (8%)
  other arithmetic  37.3 us (4%)
  starting transfers between devices  19.2 us (2%)
  between operations  16.2 us (2%)
    unnamed x9, waiting for transfers between devices  252 us
    psum x1, blocking collectives, shards(): square_total = lax.psum(local_square, ('dp', 'mp'))  230 us
    psum x1, blocking collectives, shards(): lax.psum(0.5 * jnp.sum(row_error * row_error) / all_rows, ('dp', 'mp'))  205 us
    reduce_scatter x1, waiting for transfers between devices, shards(): lax.psum_scatter(grad_in, ('dp', 'mp'), scatter_dimension=1, tiled=True)  96.1 us
    dot_general x4, matrix products, right_product(): lax.dot_general(first, second, (((1,), (1,)), ((), ())), preferred_elemen...  33.3 us
    dot_general x4, matrix products, left_product(): lax.dot_general(first, second, (((0,), (0,)), ((), ())), preferred_elemen...  32.8 us
    dot_general x4, matrix products, shards(): projected = jnp.dot(hidden, matrix, preferred_element_type=jnp.float32)  28.4 us
    gather x1, local copies, waits for them, and re-layouts, shards(): grad_states = came_back.reshape(slot_count, feat_width)[slot_index]  21.6 us
  transfers between devices with their start and end apart: 9, of which 3 were waited for; matrix products, arithmetic and copies ran while one was open for 11% of the time, Pallas kernels for 0%

commit v1 on v0

v1 whole, which is shorter than its diff:
```python
import functools

import jax
import jax.numpy as jnp
from jax import lax
from jax.experimental import pallas as pl
from jax.experimental.pallas import tpu as pltpu
from jax.sharding import PartitionSpec as P

BF = jnp.bfloat16
F32 = jnp.float32
TILES = 8
STEP = 32
VMEM = 48 * 1024 * 1024


def dot(first, second, dims):
    return lax.dot_general(first, second, (dims, ((), ())), preferred_element_type=F32)


def xor_pairs(count, bits):
    return [(i, i ^ bits) for i in range(count)]


def goal_forward_kernel(order, _, goals_ref, weight_ref, *out_refs):
    step = pl.program_id(0)
    product = dot(goals_ref[...], weight_ref[...], ((1,), (0,))).astype(BF)
    for place, out_ref in enumerate(out_refs):

        @pl.when(step == place)
        def _():
            out_ref[...] = product


def goal_forward(own, goals, weight, tiles):
    rows, width, units = goals.shape[0] // TILES, goals.shape[1], weight.shape[1]
    places = jnp.array(tiles, jnp.int32) ^ own
    return pl.pallas_call(
        functools.partial(goal_forward_kernel, tiles),
        out_shape=[jax.ShapeDtypeStruct((rows, units), BF)] * len(tiles),
        grid_spec=pltpu.PrefetchScalarGridSpec(
            num_scalar_prefetch=1,
            grid=(len(tiles),),
            in_specs=[
                pl.BlockSpec((rows, width), lambda i, places: (places[i], 0)),
                pl.BlockSpec((width, units), lambda i, places: (0, 0)),
            ],
            out_specs=[pl.BlockSpec((rows, units), lambda i, places: (0, 0))] * len(tiles),
        ),
        compiler_params=pltpu.CompilerParams(vmem_limit_bytes=VMEM),
        cost_estimate=pl.CostEstimate(
            flops=2 * len(tiles) * rows * width * units,
            bytes_accessed=len(tiles) * rows * (width + units) * 2 + width * units * 2,
            transcendentals=0,
        ),
        name="goal_forward",
    )(places, goals, weight)


def goal_backward_kernel(count, has_before, places_ref, *refs):
    grad_refs, refs = refs[:count], refs[count:]
    goals_ref, weight_ref = refs[:2]
    refs = refs[2:]
    if has_before:
        sum_before_ref = refs[1]
        refs = refs[2:]
    out_ref, sum_ref, grad_scratch = refs
    step = pl.program_id(0)
    for place in range(count):

        @pl.when(step == place)
        def _():
            grad_scratch[...] = grad_refs[place][...]

    grad = grad_scratch[...]
    out_ref[...] = dot(grad, weight_ref[...], ((1,), (1,))).astype(BF)
    share = dot(grad, goals_ref[...], ((0,), (0,)))

    @pl.when(step == 0)
    def _():
        if has_before:
            sum_ref[...] = sum_before_ref[...] + share
        else:
            sum_ref[...] = share

    @pl.when(step > 0)
    def _():
        sum_ref[...] += share


def goal_backward(own, grads, goals, weight, tiles, before):
    rows, width, units = goals.shape[0] // TILES, goals.shape[1], weight.shape[1]
    places = jnp.array(tiles, jnp.int32) ^ own
    count = len(tiles)
    whole = pl.BlockSpec((rows, units), lambda i, places: (0, 0))
    in_specs = [whole] * count + [
        pl.BlockSpec((rows, width), lambda i, places: (places[i], 0)),
        pl.BlockSpec((width, units), lambda i, places: (0, 0)),
    ]
    operands = [*grads, goals, weight]
    aliases = {}
    if before is not None:
        in_specs += [
            pl.BlockSpec(memory_space=pl.ANY),
            pl.BlockSpec((units, width), lambda i, places: (0, 0)),
        ]
        operands += list(before)
        aliases = {count + 3: 0}
    return pl.pallas_call(
        functools.partial(goal_backward_kernel, count, before is not None),
        out_shape=[
            jax.ShapeDtypeStruct(goals.shape, BF),
            jax.ShapeDtypeStruct((units, width), F32),
        ],
        grid_spec=pltpu.PrefetchScalarGridSpec(
            num_scalar_prefetch=1,
            grid=(count,),
            in_specs=in_specs,
            out_specs=[
                pl.BlockSpec((rows, width), lambda i, places: (places[i], 0)),
                pl.BlockSpec((units, width), lambda i, places: (0, 0)),
            ],
            scratch_shapes=[pltpu.VMEM((rows, units), BF)],
        ),
        input_output_aliases=aliases,
        compiler_params=pltpu.CompilerParams(vmem_limit_bytes=VMEM),
        cost_estimate=pl.CostEstimate(
            flops=4 * count * rows * width * units,
            bytes_accessed=count * rows * (2 * width + units) * 2 + width * units * 6,
            transcendentals=0,
        ),
        name="goal_backward",
    )(places, *operands)


def critic_kernel(
    count, first_tile, layers, key_ref, target_ref, states_ref, hidden_ref, vectors_ref, out_weight_ref, *refs
):
    goal_refs, refs = refs[:count], refs[count:]
    first_refs, refs = refs[:count], refs[count:]
    acts_ref, grads_ref, sums_ref, work, nhat, slope, spread, top_act, low_grad, sums = refs
    step = pl.program_id(0)
    rows, units = work.shape
    tokens = key_ref.shape[1]
    steps = rows // STEP

    @pl.when(step == 0)
    def _():
        sums[...] = jnp.zeros_like(sums)

    for place in range(count):

        @pl.when(step == place)
        def _():
            low_grad[...] = goal_refs[place][...]

    base = (first_tile + step) * rows
    slot = base + lax.broadcasted_iota(jnp.int32, (rows, tokens), 0)
    pick = (slot == key_ref[...]).astype(F32).astype(BF)
    work[...] = dot(pick, states_ref[...], ((1,), (0,))) + low_grad[...].astype(F32)

    for layer in range(layers):
        gain = vectors_ref[pl.ds(layer, 1), :]
        shift = vectors_ref[pl.ds(layers + layer, 1), :]

        @pl.loop(0, steps)
        def _(i):
            here = pl.ds(pl.multiple_of(i * STEP, STEP), STEP)
            values = work[here, :]
            center = values - jnp.mean(values, axis=1, keepdims=True)
            inverse = lax.rsqrt(jnp.mean(center * center, axis=1, keepdims=True) + 1e-05)
            scaled = center * inverse
            shifted = scaled * gain + shift
            slopes = jnp.exp(jnp.minimum(shifted, 0.0))
            nhat[layer, here, :] = scaled
            slope[layer, here, :] = slopes
            spread[layer, here, :] = inverse
            act = (jnp.maximum(shifted, 0.0) + (slopes - 1.0)).astype(BF)
            if layer < layers - 1:
                acts_ref[layer, here, :] = act
            else:
                top_act[here, :] = act

        if layer < layers - 1:
            work[...] = dot(acts_ref[layer], hidden_ref[layer], ((1,), (0,)))

    out_weight = out_weight_ref[...]
    last = top_act[...]
    value = dot(out_weight, last, ((1,), (1,)))
    target = target_ref[0]
    error = (value[0:1, :] - target[0:1, :]) * target[1:2, :]
    grad_value = (error * target[2:3, :]).astype(BF)
    grad_rows = jnp.concatenate([grad_value.astype(F32), jnp.zeros((7, rows), F32)], axis=0).astype(BF)
    sums[2 * layers] += dot(grad_rows, last, ((1,), (0,)))
    sums[2 * layers + 1] += jnp.broadcast_to(jnp.sum(error * error, axis=1, keepdims=True), (8, units))
    work[...] = dot(grad_rows, out_weight, ((0,), (0,)))

    for layer in reversed(range(layers)):
        gain = vectors_ref[pl.ds(layer, 1), :]

        @pl.loop(0, steps)
        def _(i):
            here = pl.ds(pl.multiple_of(i * STEP, STEP), STEP)
            scaled = nhat[layer, here, :]
            grad_norm = work[here, :] * slope[layer, here, :]
            by_scaled = grad_norm * scaled
            sums[layer] += jnp.sum(by_scaled.reshape(STEP // 8, 8, units), axis=0)
            sums[layers + layer] += jnp.sum(grad_norm.reshape(STEP // 8, 8, units), axis=0)
            grad_scaled = grad_norm * gain
            first_mean = jnp.mean(grad_scaled, axis=1, keepdims=True)
            second_mean = jnp.mean(by_scaled * gain, axis=1, keepdims=True)
            grad = spread[layer, here, :] * (grad_scaled - first_mean - scaled * second_mean)
            if layer > 0:
                grads_ref[layer - 1, here, :] = grad.astype(BF)
            else:
                low_grad[here, :] = grad.astype(BF)

        if layer > 0:
            work[...] = dot(grads_ref[layer - 1], hidden_ref[layer - 1], ((1,), (1,)))

    for place in range(count):

        @pl.when(step == place)
        def _():
            first_refs[place][...] = low_grad[...]

    @pl.when(step == count - 1)
    def _():
        sums_ref[...] = sums[...]


def critic(key_row, targets, state_part, hidden, vectors, out_weight, goal_parts, tiles):
    count, first_tile = len(tiles), tiles[0]
    rows, units = goal_parts[0].shape
    layers = hidden.shape[0] + 1
    whole = lambda shape: pl.BlockSpec(shape, lambda i: (0,) * len(shape))
    sums_shape = (2 * layers + 2, 8, units)
    return pl.pallas_call(
        functools.partial(critic_kernel, count, first_tile, layers),
        grid=(count,),
        out_shape=[jax.ShapeDtypeStruct((rows, units), BF)] * count
        + [jax.ShapeDtypeStruct((layers - 1, count * rows, units), BF)] * 2
        + [jax.ShapeDtypeStruct(sums_shape, F32)],
        in_specs=[
            whole(key_row.shape),
            pl.BlockSpec((1,) + targets.shape[1:], lambda i: (first_tile + i, 0, 0)),
            whole(state_part.shape),
            whole(hidden.shape),
            whole(vectors.shape),
            whole(out_weight.shape),
        ]
        + [whole((rows, units))] * count,
        out_specs=[whole((rows, units))] * count
        + [pl.BlockSpec((layers - 1, rows, units), lambda i: (0, i, 0))] * 2
        + [whole(sums_shape)],
        scratch_shapes=[
            pltpu.VMEM((rows, units), F32),
            pltpu.VMEM((layers, rows, units), F32),
            pltpu.VMEM((layers, rows, units), F32),
            pltpu.VMEM((layers, rows, 1), F32),
            pltpu.VMEM((rows, units), BF),
            pltpu.VMEM((rows, units), BF),
            pltpu.VMEM(sums_shape, F32),
        ],
        compiler_params=pltpu.CompilerParams(vmem_limit_bytes=VMEM),
        cost_estimate=pl.CostEstimate(
            flops=2 * count * rows * units * (key_row.shape[1] + 6 * units + 200),
            bytes_accessed=count * rows * units * 16 + state_part.size * 2 + hidden.size * 2,
            transcendentals=count * rows * units * layers,
        ),
        name="critic",
    )(key_row, targets, state_part, hidden, vectors, out_weight, *goal_parts)


def across(block, tile, dp_count):
    per = dp_count // TILES
    moved = block if tile == 0 else lax.ppermute(block, "dp", xor_pairs(dp_count, tile * per))
    if per == 1:
        return moved
    groups = [[group * per + low for low in range(per)] for group in range(TILES)]
    parts = moved.reshape((per, block.shape[0] // per) + block.shape[1:])
    parts = lax.all_to_all(parts, "dp", 0, 0, axis_index_groups=groups, tiled=True)
    return parts.reshape(block.shape)


def gather_pieces(piece, mp_count):
    upper = mp_count // 2
    pieces = [piece] + [None] * (mp_count - 1)
    bit = upper
    filled = [0]
    while bit:
        for j in list(filled):
            pieces[j ^ bit] = lax.ppermute(pieces[j], "mp", xor_pairs(mp_count, bit))
        filled += [j ^ bit for j in filled]
        bit //= 2
    return pieces


def piece_of(pieces, shard, own):
    return lax.select_n(own, *[pieces[shard ^ i] for i in range(len(pieces))])


def scatter_sum(partial, dp_count, mp_count):
    own_dp, own_mp = lax.axis_index("dp"), lax.axis_index("mp")
    units, width = partial.shape
    share = units // (dp_count * mp_count)
    bits = mp_count.bit_length() - 1
    held = partial.reshape((dp_count,) + (2,) * bits + (share, width))
    for level in range(bits):
        axis = bits - level
        mine = (own_mp >> level) & 1
        sent = lax.dynamic_index_in_dim(held, 1 - mine, axis, keepdims=False).astype(BF)
        kept = lax.dynamic_index_in_dim(held, mine, axis, keepdims=False)
        held = kept + lax.ppermute(sent, "mp", xor_pairs(mp_count, 1 << level)).astype(F32)
    if dp_count > TILES:
        held = held.reshape(dp_count * share, width)
        return lax.psum_scatter(held, "dp", scatter_dimension=0, tiled=True)
    total = lax.dynamic_index_in_dim(held, own_dp, 0, keepdims=False)
    sent = [lax.dynamic_index_in_dim(held, own_dp ^ o, 0, keepdims=False).astype(BF) for o in range(1, dp_count)]
    for offset, block in enumerate(sent, 1):
        total = total + lax.ppermute(block, "dp", xor_pairs(dp_count, offset)).astype(F32)
    return total


def sum_over_all(value, dp_count, mp_count):
    for name, count in (("mp", mp_count), ("dp", dp_count)):
        if count > TILES:
            value = lax.psum(value, name)
            continue
        got = [lax.ppermute(value, name, xor_pairs(count, offset)) for offset in range(1, count)]
        for other in got:
            value = value + other
    return value


def shards(
    states, dest_device, goals, returns, weight_in, weight_hidden, norm_gain, norm_shift, weight_out
):
    dp_count, mp_count = lax.axis_size("dp"), lax.axis_size("mp")
    own_dp, own_mp = lax.axis_index("dp"), lax.axis_index("mp")
    tokens, feat_width = states.shape
    all_rows = tokens * dp_count * mp_count
    slot_count, goal_width = goals.shape
    capacity = slot_count // dp_count
    shard_in, units = weight_in.shape
    layers = norm_gain.shape[0]
    shard_units = norm_gain.shape[1]
    per = dp_count // TILES
    rows = slot_count // TILES
    own_tile = own_dp // per

    cut = feat_width % shard_in
    first_goal_shard = feat_width // shard_in
    tail_pieces = gather_pieces(weight_in[cut:], mp_count)
    head_pieces = gather_pieces(weight_in[:cut], mp_count) if cut else None
    small = jnp.concatenate([norm_gain, norm_shift, weight_out[None, :]], axis=0)
    small = jnp.pad(small, ((0, 16 - small.shape[0]), (0, 0)))
    layer_pieces = gather_pieces(weight_hidden.reshape((layers - 1) * shard_units, units), mp_count)
    small_pieces = gather_pieces(small, mp_count)

    state_weight, goal_weight = [], []
    for shard in range(mp_count):
        tail = piece_of(tail_pieces, shard, own_mp)
        head = piece_of(head_pieces, shard, own_mp) if cut else None
        if shard < first_goal_shard:
            state_weight += [head, tail] if cut else [tail]
        elif shard == first_goal_shard and cut:
            state_weight.append(head)
            goal_weight.append(tail)
        else:
            goal_weight += [head, tail] if cut else [tail]
    state_weight = jnp.concatenate(state_weight, axis=0)
    goal_weight = jnp.concatenate(goal_weight, axis=0)
    hidden = jnp.concatenate(
        [
            piece_of(layer_pieces, shard, own_mp).reshape(layers - 1, shard_units, units)
            for shard in range(mp_count)
        ],
        axis=1,
    )
    vectors_bf = jnp.concatenate([piece_of(small_pieces, shard, own_mp) for shard in range(mp_count)], axis=1)
    vectors = vectors_bf.astype(F32)
    out_weight = jnp.pad(vectors_bf[2 * layers : 2 * layers + 1], ((0, 7), (0, 0)))

    dest = dest_device[:, 0]
    offset = ((dest // per) ^ own_tile) * per + dest % per
    blocks = tokens // 128
    marks = (offset[None, :] == jnp.arange(dp_count, dtype=jnp.int32)[:, None]).astype(F32)
    marks = marks.reshape(dp_count, blocks, 128)
    upper = jnp.arange(128)[:, None] < jnp.arange(128)[None, :]
    within = dot(marks.astype(BF), upper.astype(BF), ((2,), (0,)))
    block_sums = jnp.sum(marks, axis=2)
    earlier = jnp.arange(blocks)[None, :] < jnp.arange(blocks)[:, None]
    ahead = jnp.sum(jnp.where(earlier[None], block_sums[:, None, :], 0.0), axis=2)
    rank = jnp.sum(marks * (within + ahead[:, :, None]), axis=0).reshape(tokens)
    key = offset * capacity + rank.astype(jnp.int32)
    filled = jnp.sum(block_sums, axis=1)

    tile_returns = returns.reshape(TILES, rows)
    got_returns = [
        across(lax.dynamic_index_in_dim(tile_returns, own_tile ^ t, 0, keepdims=False), t, dp_count)
        for t in range(TILES)
    ]
    got_returns = jnp.stack(got_returns).reshape(dp_count, capacity).astype(F32)
    valid = (jnp.arange(capacity, dtype=F32)[None, :] < filled[:, None]).astype(F32)
    local_square = jnp.sum(valid * got_returns * got_returns)
    square_total = sum_over_all(jnp.full((8, 128), local_square), dp_count, mp_count)[0, 0]
    scale_value = jnp.sqrt(square_total / all_rows + 1e-06)
    targets = jnp.stack(
        [got_returns / scale_value, valid, jnp.full_like(valid, 1.0 / all_rows)]
        + [jnp.zeros_like(valid)] * 5
    )
    targets = targets.reshape(8, TILES, rows).transpose(1, 0, 2)

    far, near = tuple(range(TILES // 2, TILES)), tuple(range(TILES // 2))
    sent_far = goal_forward(own_tile, goals, goal_weight, far)
    got_far = [across(block, tile, dp_count) for block, tile in zip(sent_far, far)]
    sent_near = goal_forward(own_tile, goals, goal_weight, near)
    got_near = [across(block, tile, dp_count) for block, tile in zip(sent_near, near)]

    state_part = dot(states, state_weight, ((1,), (0,))).astype(BF)
    key_row = key[None, :]
    half = len(far) // 2
    groups = ((near, got_near), (far[:half], got_far[:half]), (far[half:], got_far[half:]))
    first_grads, acts, grads, sums = [], [], [], []
    for tiles, got in groups:
        made = critic(key_row, targets, state_part, hidden, vectors, out_weight, got, tiles)
        first_grads.append(made[: len(tiles)])
        acts.append(made[-3])
        grads.append(made[-2])
        sums.append(made[-1])
    back = [
        [across(block, tile, dp_count) for block, tile in zip(blocks_of, tiles)]
        for blocks_of, (tiles, _) in zip(first_grads, groups)
    ]

    all_first = jnp.concatenate([block for blocks_of in first_grads for block in blocks_of], axis=0)
    pick = (key[:, None] == jnp.arange(slot_count, dtype=jnp.int32)[None, :]).astype(BF)
    first_grad = dot(pick, all_first, ((1,), (0,))).astype(BF)
    grad_states = dot(first_grad, state_weight, ((1,), (1,))).astype(BF)
    grad_state_weight = dot(first_grad, states, ((0,), (0,)))
    grad_hidden = [
        sum(dot(grad[layer], act[layer], ((0,), (0,))) for grad, act in zip(grads, acts))
        for layer in range(layers - 1)
    ]
    sums = sum(sums)
    vector_sums = jnp.sum(sums[: 2 * layers + 1], axis=1)
    local_loss = 0.5 * sums[2 * layers + 1, 0, 0] / all_rows
    vector_sums = jnp.concatenate([vector_sums, jnp.full((1, units), local_loss)], axis=0)
    high = vector_sums.astype(BF).astype(F32)
    count = 2 * layers + 2
    columns = jnp.concatenate(
        [high, vector_sums - high, jnp.zeros((128 - 2 * count, units), F32)], axis=0
    ).T
    share = scatter_sum(
        jnp.concatenate([grad_state_weight] + grad_hidden + [columns], axis=1), dp_count, mp_count
    )
    vector_share = share[:, -128:]
    vector_share = (vector_share[:, :count] + vector_share[:, count : 2 * count]).T

    running = None
    for (tiles, _), got in zip(groups, back):
        running = goal_backward(own_tile, got, goals, goal_weight, tiles, running)
    grad_goals, grad_goal_weight = running
    goal_share = scatter_sum(grad_goal_weight, dp_count, mp_count)

    state_share = share[:, :feat_width]
    hidden_share = share[:, feat_width : feat_width + (layers - 1) * units]
    return (
        vector_share[count - 1, 0],
        grad_states,
        grad_goals,
        jnp.concatenate([state_share, goal_share], axis=1).T,
        hidden_share.reshape(-1, layers - 1, units).transpose(1, 2, 0),
        vector_share[:layers],
        vector_share[layers : 2 * layers],
        vector_share[2 * layers],
    )


def solution(mesh):
    placed = (
        P(("dp", "mp"), None),
        P(("dp", "mp"), None),
        P(("dp", "mp"), None),
        P(("dp", "mp")),
        P("mp", None),
        P(None, "mp", None),
        P(None, "mp"),
        P(None, "mp"),
        P("mp"),
    )
    return jax.shard_map(
        shards,
        mesh=mesh,
        in_specs=placed,
        out_specs=(
            P(),
            P(("dp", "mp"), None),
            P(("dp", "mp"), None),
            P(None, ("dp", "mp")),
            P(None, None, ("dp", "mp")),
            P(None, ("dp", "mp")),
            P(None, ("dp", "mp")),
            P(("dp", "mp")),
        ),
        check_vma=False,
    )
```

time: 1060 us -> 433 us (0.41)
  blocking collectives: 451 us -> 0 us
  waiting for transfers between devices: 348 us -> 99.2 us
  Pallas kernels: 0 us -> 165 us
  local copies, waits for them, and re-layouts: 89.4 us -> 24.2 us
  starting transfers between devices: 19.2 us -> 83.3 us
  matrix products: 95.7 us -> 39.1 us
  other arithmetic: 37.3 us -> 13.8 us
  between operations: 16.2 us -> 3.19 us
    psum x2 -> x0, blocking collectives: 436 us -> none  [the longest x1 230 us: shards(): square_total = lax.psum(local_square, ('dp', 'mp'))]
    unnamed x9 -> x0, waiting for transfers between devices: 252 us -> none
    pallas_call x0 -> x8, Pallas kernels: none -> 165 us  [the longest x3 136 us: critic(): pl.pallas_call(functools.partial(critic_kernel, count, first_tile, layers...]
    ppermute x0 -> x61, waiting for transfers between devices: none -> 99.2 us  [the longest x21 53.8 us: across(): lax.ppermute(block, 'dp', xor_pairs(dp_count, tile * per))]
    reduce_scatter x1 -> x0, waiting for transfers between devices: 96.1 us -> none  [shards(): lax.psum_scatter(grad_in, ('dp', 'mp'), scatter_dimension=1, tiled=True)]
    ppermute x0 -> x61, starting transfers between devices: none -> 83.3 us  [the longest x21 34.2 us: across(): lax.ppermute(block, 'dp', xor_pairs(dp_count, tile * per))]
    dot_general x14, matrix products: 95.7 us -> 39.1 us  [dot(): lax.dot_general(first, second, (dims, ((), ())), preferred_element_type=F32)]
    scatter x2 -> x0, local copies, waits for them, and re-layouts: 33.8 us -> none  [the longest x1 19.2 us: shards(): jnp.zeros((slot_count, feat_width), jnp.bfloat16).at[slot_index].set(states)]
  transfers between devices with their start and end apart: 9 -> 61, of which waited for: 3 -> 19; matrix products, arithmetic and copies ran while one was open for 11% -> 8% of each run, Pallas kernels for 0% -> 22%
where the time goes in v1:
time: 433 us; the launch traced here: 428 us
  Pallas kernels  165 us (38%)
  waiting for transfers between devices  99.2 us (23%)
  starting transfers between devices  83.3 us (19%)
  matrix products  39.1 us (9%)
  local copies, waits for them, and re-layouts  24.2 us (6%)
  other arithmetic  13.8 us (3%)
    pallas_call x3, Pallas kernels, critic(): pl.pallas_call(functools.partial(critic_kernel, count, first_tile, layers...  136 us
    ppermute x21, waiting for transfers between devices, across(): lax.ppermute(block, 'dp', xor_pairs(dp_count, tile * per))  53.8 us
    dot_general x14, matrix products, dot(): lax.dot_general(first, second, (dims, ((), ())), preferred_element_type=F32)  39.1 us
    ppermute x21, starting transfers between devices, across(): lax.ppermute(block, 'dp', xor_pairs(dp_count, tile * per))  34.2 us
    ppermute x14, starting transfers between devices, scatter_sum(): lax.ppermute(block, 'dp', xor_pairs(dp_count, offset)).astype(F32)  27.3 us
    ppermute x4, waiting for transfers between devices, scatter_sum(): lax.ppermute(sent, 'mp', xor_pairs(mp_count, 1 << level)).astype(F32)  25.8 us
    pallas_call x3, Pallas kernels, goal_backward(): pl.pallas_call(functools.partial(goal_backward_kernel, count, before is n...  19 us
    unnamed x93, local copies, waits for them, and re-layouts  13.2 us
  transfers between devices with their start and end apart: 61, of which 19 were waited for; matrix products, arithmetic and copies ran while one was open for 8% of the time, Pallas kernels for 22%

profile of v1, /device:TPU:0, one launch (start us, length us, event | category | flops | bytes accessed | tf_op | source)
XLA Modules:
  0.0 427.6 jit_solution(12815536612019534050)
XLA Ops:
  1.6 6.0 %collective-permute-start.6 = (bf16[320]{0:T(512)(128)(2,1)S(1)}, bf16[320]{0:T(512)(128)(2,1)S(1)}, u32[]{:S(2)}, u32[]{:S(2)}) collective-permute-start(bf16[320]{0:T(512)(128)(2,1)S(1)} %get-tuple-element.112), channel_id=1, source_target_pairs={{0,28},{4,24},{8,20},{12,16},{16,12},{20,8},{24,4},{28,0},{1,29},{... | collective-permute-start | bytes 1928 | tf_op jit(solution)/shard_map/ppermute | solution.py:277
  10.6 2.3 collective-permute-start.2
  31.5 3.6 collective-permute-start.16
  51.5 4.6 %collective-permute-done.21 = bf16[256,512]{1,0:T(8,128)(2,1)S(1)} collective-permute-done((bf16[256,512]{1,0:T(8,128)(2,1)S(1)}, bf16[256,512]{1,0:T(8,128)(2,1)S(1)}, u32[]{:S(2)}, u32[]{:S(2)}) %collective-permute-start.21) | collective-permute-done | bytes 262176 | tf_op jit(solution)/shard_map/ppermute | solution.py:293
  60.3 5.0 %goal_forward.3 = (bf16[320,512]{1,0:T(8,128)(2,1)S(1)}, bf16[320,512]{1,0:T(8,128)(2,1)S(1)}, bf16[320,512]{1,0:T(8,128)(2,1)S(1)}, bf16[320,512]{1,0:T(8,128)(2,1)S(1)}) custom-call(s32[4]{0:T(128)S(1)} %get-tuple-element.153._, bf16[2560,1024]{1,0:T(8,128)(2,1)} %refs_2_.3, bf16[1024,512]{1,0:T(8,128)(2,1)S(1)} %pad_maximum_fusion.1.weight_ref.refs_5_.refs_3_), custom_call_target="tpu_custom_call" | custom-call | flops 1342177280 | bytes 4980736 | tf_op jit(solution)/shard_map/goal_forward/pallas_call | solution.py:38
  65.3 2.3 collective-permute-start.32
  68.3 3.6 collective-permute-start.34
  73.0 4.4 %goal_forward.2 = (bf16[320,512]{1,0:T(8,128)(2,1)S(1)}, bf16[320,512]{1,0:T(8,128)(2,1)S(1)}, bf16[320,512]{1,0:T(8,128)(2,1)S(1)}, bf16[320,512]{1,0:T(8,128)(2,1)S(1)}) custom-call(s32[4]{0:T(128)S(1)} %get-tuple-element.152._.places_ref, bf16[2560,1024]{1,0:T(8,128)(2,1)} %refs_2_.3, bf16[1024,512]{1,0:T(8,128)(2,1)S(1)} %pad_maximum_fusion.1.weight_ref.refs_5_.refs_3_), custom_call_target="tpu_custom_call" | custom-call | flops 1342177280 | bytes 4980736 | tf_op jit(solution)/shard_map/goal_forward/pallas_call | solution.py:38
  78.1 9.1 %fusion.3.states_ref = bf16[2048,512]{1,0:T(8,128)(2,1)} fusion(bf16[2048,2048]{1,0:T(8,128)(2,1)} %param.14, bf16[2048,512]{1,0:T(8,128)(2,1)S(1)} %get-tuple-element.122), kind=kOutput, calls=%fused_computation.9 | convolution fusion | flops 4296015872 | bytes 12582912 | tf_op jit(solution)/shard_map/dot_general | solution.py:18
  87.2 17.7 %collective-permute-done.32.refs_0_ = bf16[320,512]{1,0:T(8,128)(2,1)S(1)} collective-permute-done((bf16[320,512]{1,0:T(8,128)(2,1)S(1)}, bf16[320,512]{1,0:T(8,128)(2,1)S(1)}, u32[]{:S(2)}, u32[]{:S(2)}) %collective-permute-start.32) | collective-permute-done | bytes 327712 | tf_op jit(solution)/shard_map/ppermute | solution.py:277
  104.9 7.1 %collective-permute-done.33.refs_1_ = bf16[320,512]{1,0:T(8,128)(2,1)S(1)} collective-permute-done((bf16[320,512]{1,0:T(8,128)(2,1)S(1)}, bf16[320,512]{1,0:T(8,128)(2,1)S(1)}, u32[]{:S(2)}, u32[]{:S(2)}) %collective-permute-start.33) | collective-permute-done | bytes 327712 | tf_op jit(solution)/shard_map/ppermute | solution.py:277
  112.0 34.6 %critic.4 = (bf16[320,512]{1,0:T(8,128)(2,1)}, bf16[320,512]{1,0:T(8,128)(2,1)S(1)}, bf16[3,640,512]{2,1,0:T(8,128)(2,1)S(1)}, bf16[3,640,512]{2,1,0:T(8,128)(2,1)}, f32[10,8,512]{2,1,0:T(8,128)S(1)}) custom-call(s32[1,2048]{1,0:T(1,128)S(1)} %bitcast_add_fusion.6.key_ref, f32[8,8,320]{2,1,0:T(8,128)S(1)} %bitcast.181, bf16[2048,512]{1,0:T(8,128)(2,1)} %fusion.3.states_ref, ...), custom_call_target="tpu_custom_call" | custom-call | flops 3486515200 | bytes 8912896 | tf_op jit(solution)/shard_map/critic/pallas_call | solution.py:238
  149.7 34.6 %critic.5 = (bf16[320,512]{1,0:T(8,128)(2,1)S(1)}, bf16[320,512]{1,0:T(8,128)(2,1)S(1)}, bf16[3,640,512]{2,1,0:T(8,128)(2,1)S(1)}, bf16[3,640,512]{2,1,0:T(8,128)(2,1)}, f32[10,8,512]{2,1,0:T(8,128)S(1)}) custom-call(s32[1,2048]{1,0:T(1,128)S(1)} %bitcast_add_fusion.6.key_ref, f32[8,8,320]{2,1,0:T(8,128)S(1)} %bitcast.182, ...), custom_call_target="tpu_custom_call" | custom-call | flops 3486515200 | bytes 8912896 | tf_op jit(solution)/shard_map/critic/pallas_call | solution.py:238
  185.1 67.1 %critic.3 = (bf16[320,512]{1,0:T(8,128)(2,1)S(1)}, bf16[320,512]{1,0:T(8,128)(2,1)S(1)}, bf16[320,512]{1,0:T(8,128)(2,1)S(1)}, bf16[320,512]{1,0:T(8,128)(2,1)},...) custom-call(s32[1,2048]{1,0:T(1,128)S(1)} %bitcast_add_fusion.6.key_ref, ...), custom_call_target="tpu_custom_call" | custom-call | flops 6973030400 | bytes 14155776 | tf_op jit(solution)/shard_map/critic/pallas_call | solution.py:238
  253.6 3.7 convolution_add_fusion.3
  268.9 6.1 %fusion.2 = bf16[2048,512]{1,0:T(8,128)(2,1)S(1)} fusion(bf16[2560,512]{1,0:T(8,128)(2,1)S(1)} %constant_dynamic-update-slice_fusion.8, s32[2048]{0:T(1024)S(1)} %bitcast.199), kind=kOutput, calls=%fused_computation.8 | convolution fusion | flops 5375000576 | bytes 4726784 | tf_op jit(solution)/shard_map/dot_general | solution.py:18
  275.1 4.6 %convolution_dynamic-update-slice_fusion = f32[512,3712]{1,0:T(8,128)S(1)} fusion(bf16[2048,512]{1,0:T(8,128)(2,1)S(1)} %fusion.2, bf16[2048,2048]{1,0:T(8,128)(2,1)S(1)} %bitcast.203), kind=kOutput, calls=%fused_computation.6 | convolution fusion | flops 4294967296 | bytes 14680064 | tf_op jit(solution)/shard_map/dot_general | solution.py:18
  289.3 2.8 collective-permute-start.47
  292.1 2.9 collective-permute-done.49.refs_1_
  295.8 3.7 collective-permute-start.48
  299.5 10.0 %collective-permute-done.50.refs_2_ = bf16[320,512]{1,0:T(8,128)(2,1)} collective-permute-done((bf16[320,512]{1,0:T(8,128)(2,1)S(1)}, bf16[320,512]{1,0:T(8,128)(2,1)}, u32[]{:S(2)}, u32[]{:S(2)}) %collective-permute-start.50) | collective-permute-done | bytes 327712 | tf_op jit(solution)/shard_map/ppermute | solution.py:277
  311.2 6.8 %collective-permute-done.51.refs_3_ = bf16[320,512]{1,0:T(8,128)(2,1)} collective-permute-done((bf16[320,512]{1,0:T(8,128)(2,1)}, bf16[320,512]{1,0:T(8,128)(2,1)}, u32[]{:S(2)}, u32[]{:S(2)}) %collective-permute-start.51) | collective-permute-done | bytes 327712 | tf_op jit(solution)/shard_map/ppermute | solution.py:277
  319.7 8.1 %goal_backward.3 = (bf16[2560,1024]{1,0:T(8,128)(2,1)}, f32[512,1024]{1,0:T(8,128)S(1)}) custom-call(s32[4]{0:T(128)S(1)} %get-tuple-element.152._.places_ref, bf16[320,512]{1,0:T(8,128)(2,1)S(1)} %copy-done.7, bf16[320,512]{1,0:T(8,128)(2,1)S(1)} %copy-done.13, bf16[320,512]{1,0:T(8,128)(2,1)} %collective-permute-done.50.refs_2_, ...), custom_call_target="tpu_custom_call" | custom-call | flops 2684354560 | bytes 9699328 | tf_op jit(solution)/shard_map/goal_backward/pallas_call | solution.py:109
  327.8 8.1 %collective-permute-done.48.refs_1_ = bf16[320,512]{1,0:T(8,128)(2,1)S(1)} collective-permute-done((bf16[320,512]{1,0:T(8,128)(2,1)S(1)}, bf16[320,512]{1,0:T(8,128)(2,1)S(1)}, u32[]{:S(2)}, u32[]{:S(2)}) %collective-permute-start.48) | collective-permute-done | bytes 327712 | tf_op jit(solution)/shard_map/ppermute | solution.py:277
  335.9 5.2 %goal_backward.4 = (bf16[2560,1024]{1,0:T(8,128)(2,1)}, f32[512,1024]{1,0:T(8,128)S(1)}) custom-call(s32[2]{0:T(128)S(1)} %broadcast_xor_fusion.1.places_ref, bf16[320,512]{1,0:T(8,128)(2,1)S(1)} %collective-permute-done.47.refs_0_, bf16[320,512]{1,0:T(8,128)(2,1)S(1)} %collective-permute-done.48.refs_1_, ...), custom_call_target="tpu_custom_call", output_to_operand_aliasing={{0}: (5, {})} | custom-call | flops 1342177280 | bytes 6422528 | tf_op jit(solution)/shard_map/goal_backward/pallas_call | solution.py:109
  341.1 5.7 %goal_backward.5 = (bf16[2560,1024]{1,0:T(8,128)(2,1)}, f32[512,1024]{1,0:T(8,128)S(1)}) custom-call(s32[2]{0:T(128)S(1)} %broadcast_xor_fusion.2.places_ref, bf16[320,512]{1,0:T(8,128)(2,1)S(1)} %collective-permute-done.45.refs_0_, bf16[320,512]{1,0:T(8,128)(2,1)S(1)} %collective-permute-done.46.refs_1_, ...), custom_call_target="tpu_custom_call", output_to_operand_aliasing={{0}: (5, {})} | custom-call | flops 1342177280 | bytes 6422528 | tf_op jit(solution)/shard_map/goal_backward/pallas_call | solution.py:109
  352.5 25.7 %collective-permute-done.53 = bf16[8,16,1024]{2,1,0:T(8,128)(2,1)S(1)} collective-permute-done((bf16[8,16,1024]{2,1,0:T(8,128)(2,1)S(1)}, bf16[8,16,1024]{2,1,0:T(8,128)(2,1)S(1)}, u32[]{:S(2)}, u32[]{:S(2)}) %collective-permute-start.53) | collective-permute-done | bytes 262176 | tf_op jit(solution)/shard_map/ppermute | solution.py:314
  380.3 2.2 collective-permute-start.60
  383.7 8.6 %collective-permute-start.58 = (bf16[16,1024]{1,0:T(8,128)(2,1)S(1)}, bf16[16,1024]{1,0:T(8,128)(2,1)S(1)}, u32[]{:S(2)}, u32[]{:S(2)}) collective-permute-start(bf16[16,1024]{1,0:T(8,128)(2,1)S(1)} %get-tuple-element.140), channel_id=1, source_target_pairs={{0,20},{4,16},{8,28},{12,24},{16,4},{20,0},{24,12},{28,8},{1,21},{... | collective-permute-start | bytes 98312 | tf_op jit(solution)/shard_map/ppermute | solution.py:321
  398.0 2.2 collective-permute-start.44
  400.2 6.8 %convolution_convert_fusion = bf16[2048,2048]{1,0:T(8,128)(2,1)} fusion(bf16[2048,512]{1,0:T(8,128)(2,1)S(1)} %copy-done.33, bf16[2048,512]{1,0:T(8,128)(2,1)S(1)} %copy-done.26), kind=kOutput, calls=%fused_computation.3 | convolution fusion | flops 4299161600 | bytes 12582912 | tf_op jit(solution)/shard_map/dot_general | solution.py:18
  415.0 7.6 %collective-permute-done.42 = bf16[16,3712]{1,0:T(8,128)(2,1)S(1)} collective-permute-done((bf16[16,3712]{1,0:T(8,128)(2,1)S(1)}, bf16[16,3712]{1,0:T(8,128)(2,1)S(1)}, u32[]{:S(2)}, u32[]{:S(2)}) %collective-permute-start.42) | collective-permute-done | bytes 118816 | tf_op jit(solution)/shard_map/ppermute | solution.py:321
  (285 shorter events, 101.5 us)
Async XLA Ops:
  1.6 18.3 %collective-permute-start.6 = (bf16[320]{0:T(512)(128)(2,1)S(1)}, bf16[320]{0:T(512)(128)(2,1)S(1)}, u32[]{:S(2)}, u32[]{:S(2)}) collective-permute-start(bf16[320]{0:T(512)(128)(2,1)S(1)} %get-tuple-element.112), channel_id=1, source_target_pairs={{0,28},{4,24},{8,20},{12,16},{16,12},{20,8},{24,4},{28,0},{1,29},{... | collective-permute-start | bytes 1928 | tf_op jit(solution)/shard_map/ppermute | solution.py:277
  7.6 13.1 %collective-permute-start.5 = (bf16[320]{0:T(512)(128)(2,1)S(1)}, bf16[320]{0:T(512)(128)(2,1)S(1)}, u32[]{:S(2)}, u32[]{:S(2)}) collective-permute-start(bf16[320]{0:T(512)(128)(2,1)S(1)} %get-tuple-element.113), channel_id=1, source_target_pairs={{0,24},{4,28},{8,16},{12,20},{16,8},{20,12},{24,0},{28,4},{1,25},{... | collective-permute-start | bytes 1928 | tf_op jit(solution)/shard_map/ppermute | solution.py:277
  7.8 13.4 %collective-permute-start.4 = (bf16[320]{0:T(512)(128)(2,1)S(1)}, bf16[320]{0:T(512)(128)(2,1)S(1)}, u32[]{:S(2)}, u32[]{:S(2)}) collective-permute-start(bf16[320]{0:T(512)(128)(2,1)S(1)} %get-tuple-element.114), channel_id=1, source_target_pairs={{0,20},{4,16},{8,28},{12,24},{16,4},{20,0},{24,12},{28,8},{1,21},{... | collective-permute-start | bytes 1928 | tf_op jit(solution)/shard_map/ppermute | solution.py:277
  21.2 13.9 %collective-permute-start.26 = (bf16[16,128]{1,0:T(8,128)(2,1)S(1)}, bf16[16,128]{1,0:T(8,128)(2,1)S(1)}, u32[]{:S(2)}, u32[]{:S(2)}) collective-permute-start(bf16[16,128]{1,0:T(8,128)(2,1)S(1)} %fusion.89), channel_id=1, source_target_pairs={{0,1},{1,0},{2,3},{3,2},{4,5},{5,4},{6,7},{7,6},{8,9},{9,8},{10,11... | collective-permute-start | bytes 12296 | tf_op jit(solution)/shard_map/ppermute | solution.py:293
  27.9 20.0 %collective-permute-start.24 = (bf16[384,512]{1,0:T(8,128)(2,1)}, bf16[384,512]{1,0:T(8,128)(2,1)S(1)}, u32[]{:S(2)}, u32[]{:S(2)}) collective-permute-start(bf16[384,512]{1,0:T(8,128)(2,1)} %bitcast.193), channel_id=1, source_target_pairs={{0,2},{1,3},{2,0},{3,1},{4,6},{5,7},{6,4},{7,5},{8,10},{9,11},{10,... | collective-permute-start | bytes 1179656 | tf_op jit(solution)/shard_map/ppermute | solution.py:293
  29.5 21.8 %collective-permute-start.18 = (bf16[512,512]{1,0:T(8,128)(2,1)}, bf16[512,512]{1,0:T(8,128)(2,1)S(1)}, u32[]{:S(2)}, u32[]{:S(2)}) collective-permute-start(bf16[512,512]{1,0:T(8,128)(2,1)} %slice.100), channel_id=1, source_target_pairs={{0,2},{1,3},{2,0},{3,1},{4,6},{5,7},{6,4},{7,5},{8,10},{9,11},{10,... | collective-permute-start | bytes 1572872 | tf_op jit(solution)/shard_map/ppermute | solution.py:293
  65.3 39.6 %collective-permute-start.32 = (bf16[320,512]{1,0:T(8,128)(2,1)S(1)}, bf16[320,512]{1,0:T(8,128)(2,1)S(1)}, u32[]{:S(2)}, u32[]{:S(2)}) collective-permute-start(bf16[320,512]{1,0:T(8,128)(2,1)S(1)} %get-tuple-element.47), channel_id=1, source_target_pairs={{0,16},{4,20},{8,24},{12,28},{16,0},{20,4},{24,8},{28,12},{1,17},{... | collective-permute-start | bytes 983048 | tf_op jit(solution)/shard_map/ppermute | solution.py:277
  67.6 44.4 %collective-permute-start.33 = (bf16[320,512]{1,0:T(8,128)(2,1)S(1)}, bf16[320,512]{1,0:T(8,128)(2,1)S(1)}, u32[]{:S(2)}, u32[]{:S(2)}) collective-permute-start(bf16[320,512]{1,0:T(8,128)(2,1)S(1)} %get-tuple-element.48), channel_id=1, source_target_pairs={{0,20},{4,16},{8,28},{12,24},{16,4},{20,0},{24,12},{28,8},{1,21},{... | collective-permute-start | bytes 983048 | tf_op jit(solution)/shard_map/ppermute | solution.py:277
  68.3 81.4 %collective-permute-start.34 = (bf16[320,512]{1,0:T(8,128)(2,1)S(1)}, bf16[320,512]{1,0:T(8,128)(2,1)S(1)}, u32[]{:S(2)}, u32[]{:S(2)}) collective-permute-start(bf16[320,512]{1,0:T(8,128)(2,1)S(1)} %get-tuple-element.51), channel_id=1, source_target_pairs={{0,24},{4,28},{8,16},{12,20},{16,8},{20,12},{24,0},{28,4},{1,25},{... | collective-permute-start | bytes 983048 | tf_op jit(solution)/shard_map/ppermute | solution.py:277
  71.9 77.8 %collective-permute-start.35 = (bf16[320,512]{1,0:T(8,128)(2,1)S(1)}, bf16[320,512]{1,0:T(8,128)(2,1)S(1)}, u32[]{:S(2)}, u32[]{:S(2)}) collective-permute-start(bf16[320,512]{1,0:T(8,128)(2,1)S(1)} %get-tuple-element.52), channel_id=1, source_target_pairs={{0,28},{4,24},{8,20},{12,16},{16,12},{20,8},{24,4},{28,0},{1,29},{... | collective-permute-start | bytes 983048 | tf_op jit(solution)/shard_map/ppermute | solution.py:277
  77.5 107.6 %collective-permute-start.29 = (bf16[320,512]{1,0:T(8,128)(2,1)S(1)}, bf16[320,512]{1,0:T(8,128)(2,1)S(1)}, u32[]{:S(2)}, u32[]{:S(2)}) collective-permute-start(bf16[320,512]{1,0:T(8,128)(2,1)S(1)} %get-tuple-element.40), channel_id=1, source_target_pairs={{0,4},{4,0},{8,12},{12,8},{16,20},{20,16},{24,28},{28,24},{1,5},{5... | collective-permute-start | bytes 983048 | tf_op jit(solution)/shard_map/ppermute | solution.py:277
  104.9 80.1 %collective-permute-start.30 = (bf16[320,512]{1,0:T(8,128)(2,1)S(1)}, bf16[320,512]{1,0:T(8,128)(2,1)S(1)}, u32[]{:S(2)}, u32[]{:S(2)}) collective-permute-start(bf16[320,512]{1,0:T(8,128)(2,1)S(1)} %get-tuple-element.41), channel_id=1, source_target_pairs={{0,8},{4,12},{8,0},{12,4},{16,24},{20,28},{24,16},{28,20},{1,9},{5... | collective-permute-start | bytes 983048 | tf_op jit(solution)/shard_map/ppermute | solution.py:277
  112.0 73.1 %collective-permute-start.31 = (bf16[320,512]{1,0:T(8,128)(2,1)S(1)}, bf16[320,512]{1,0:T(8,128)(2,1)S(1)}, u32[]{:S(2)}, u32[]{:S(2)}) collective-permute-start(bf16[320,512]{1,0:T(8,128)(2,1)S(1)} %get-tuple-element.42), channel_id=1, source_target_pairs={{0,12},{4,8},{8,4},{12,0},{16,28},{20,24},{24,20},{28,16},{1,13},{... | collective-permute-start | bytes 983048 | tf_op jit(solution)/shard_map/ppermute | solution.py:277
  284.9 62.0 %collective-permute-start.36 = (bf16[8,2,16,3712]{3,2,1,0:T(8,128)(2,1)}, bf16[8,2,16,3712]{3,2,1,0:T(8,128)(2,1)}, u32[]{:S(2)}, u32[]{:S(2)}) collective-permute-start(bf16[8,2,16,3712]{3,2,1,0:T(8,128)(2,1)} %fusion.4), channel_id=1, source_target_pairs={{0,1},{1,0},{2,3},{3,2},{4,5},{5,4},{6,7},{7,6},{8,9},{9,8},{10,11... | collective-permute-start | bytes 5701640 | tf_op jit(solution)/shard_map/ppermute | solution.py:314
  286.4 23.0 %collective-permute-start.50 = (bf16[320,512]{1,0:T(8,128)(2,1)S(1)}, bf16[320,512]{1,0:T(8,128)(2,1)}, u32[]{:S(2)}, u32[]{:S(2)}) collective-permute-start(bf16[320,512]{1,0:T(8,128)(2,1)S(1)} %copy-done.9), channel_id=1, source_target_pairs={{0,8},{4,12},{8,0},{12,4},{16,24},{20,28},{24,16},{28,20},{1,9},{5... | collective-permute-start | bytes 983048 | tf_op jit(solution)/shard_map/ppermute | solution.py:277
  288.4 29.5 %collective-permute-start.51 = (bf16[320,512]{1,0:T(8,128)(2,1)}, bf16[320,512]{1,0:T(8,128)(2,1)}, u32[]{:S(2)}, u32[]{:S(2)}) collective-permute-start(bf16[320,512]{1,0:T(8,128)(2,1)} %get-tuple-element.46), channel_id=1, source_target_pairs={{0,12},{4,8},{8,4},{12,0},{16,28},{20,24},{24,20},{28,16},{1,13},{... | collective-permute-start | bytes 983048 | tf_op jit(solution)/shard_map/ppermute | solution.py:277
  289.3 38.4 %collective-permute-start.47 = (bf16[320,512]{1,0:T(8,128)(2,1)}, bf16[320,512]{1,0:T(8,128)(2,1)S(1)}, u32[]{:S(2)}, u32[]{:S(2)}) collective-permute-start(bf16[320,512]{1,0:T(8,128)(2,1)} %get-tuple-element.49), channel_id=1, source_target_pairs={{0,16},{4,20},{8,24},{12,28},{16,0},{20,4},{24,8},{28,12},{1,17},{... | collective-permute-start | bytes 983048 | tf_op jit(solution)/shard_map/ppermute | solution.py:277
  295.8 40.1 %collective-permute-start.48 = (bf16[320,512]{1,0:T(8,128)(2,1)S(1)}, bf16[320,512]{1,0:T(8,128)(2,1)S(1)}, u32[]{:S(2)}, u32[]{:S(2)}) collective-permute-start(bf16[320,512]{1,0:T(8,128)(2,1)S(1)} %get-tuple-element.50), channel_id=1, source_target_pairs={{0,20},{4,16},{8,28},{12,24},{16,4},{20,0},{24,12},{28,8},{1,21},{... | collective-permute-start | bytes 983048 | tf_op jit(solution)/shard_map/ppermute | solution.py:277
  309.5 31.6 %collective-permute-start.45 = (bf16[320,512]{1,0:T(8,128)(2,1)S(1)}, bf16[320,512]{1,0:T(8,128)(2,1)S(1)}, u32[]{:S(2)}, u32[]{:S(2)}) collective-permute-start(bf16[320,512]{1,0:T(8,128)(2,1)S(1)} %copy-done.5), channel_id=1, source_target_pairs={{0,24},{4,28},{8,16},{12,20},{16,8},{20,12},{24,0},{28,4},{1,25},{... | collective-permute-start | bytes 983048 | tf_op jit(solution)/shard_map/ppermute | solution.py:277
  318.0 23.1 %collective-permute-start.46 = (bf16[320,512]{1,0:T(8,128)(2,1)S(1)}, bf16[320,512]{1,0:T(8,128)(2,1)S(1)}, u32[]{:S(2)}, u32[]{:S(2)}) collective-permute-start(bf16[320,512]{1,0:T(8,128)(2,1)S(1)} %copy-done.2), channel_id=1, source_target_pairs={{0,28},{4,24},{8,20},{12,16},{16,12},{20,8},{24,4},{28,0},{1,29},{... | collective-permute-start | bytes 983048 | tf_op jit(solution)/shard_map/ppermute | solution.py:277
  349.1 43.2 %collective-permute-start.37 = (bf16[8,16,3712]{2,1,0:T(8,128)(2,1)S(1)}, bf16[8,16,3712]{2,1,0:T(8,128)(2,1)S(1)}, u32[]{:S(2)}, u32[]{:S(2)}) collective-permute-start(bf16[8,16,3712]{2,1,0:T(8,128)(2,1)S(1)} %fusion.22), channel_id=1, source_target_pairs={{0,2},{1,3},{2,0},{3,1},{4,6},{5,7},{6,4},{7,5},{8,10},{9,11},{10,... | collective-permute-start | bytes 2850824 | tf_op jit(solution)/shard_map/ppermute | solution.py:314
  350.9 27.3 %collective-permute-start.53 = (bf16[8,16,1024]{2,1,0:T(8,128)(2,1)S(1)}, bf16[8,16,1024]{2,1,0:T(8,128)(2,1)S(1)}, u32[]{:S(2)}, u32[]{:S(2)}) collective-permute-start(bf16[8,16,1024]{2,1,0:T(8,128)(2,1)S(1)} %fusion.51), channel_id=1, source_target_pairs={{0,2},{1,3},{2,0},{3,1},{4,6},{5,7},{6,4},{7,5},{8,10},{9,11},{10,... | collective-permute-start | bytes 786440 | tf_op jit(solution)/shard_map/ppermute | solution.py:314
  378.3 16.0 %collective-permute-start.54 = (bf16[16,1024]{1,0:T(8,128)(2,1)S(1)}, bf16[16,1024]{1,0:T(8,128)(2,1)S(1)}, u32[]{:S(2)}, u32[]{:S(2)}) collective-permute-start(bf16[16,1024]{1,0:T(8,128)(2,1)S(1)} %get-tuple-element.137), channel_id=1, source_target_pairs={{0,4},{4,0},{8,12},{12,8},{16,20},{20,16},{24,28},{28,24},{1,5},{5... | collective-permute-start | bytes 98312 | tf_op jit(solution)/shard_map/ppermute | solution.py:321
  380.3 16.2 %collective-permute-start.60 = (bf16[16,1024]{1,0:T(8,128)(2,1)S(1)}, bf16[16,1024]{1,0:T(8,128)(2,1)S(1)}, u32[]{:S(2)}, u32[]{:S(2)}) collective-permute-start(bf16[16,1024]{1,0:T(8,128)(2,1)S(1)} %get-tuple-element.138), channel_id=1, source_target_pairs={{0,28},{4,24},{8,20},{12,16},{16,12},{20,8},{24,4},{28,0},{1,29},{... | collective-permute-start | bytes 98312 | tf_op jit(solution)/shard_map/ppermute | solution.py:321
  382.5 14.1 %collective-permute-start.59 = (bf16[16,1024]{1,0:T(8,128)(2,1)S(1)}, bf16[16,1024]{1,0:T(8,128)(2,1)S(1)}, u32[]{:S(2)}, u32[]{:S(2)}) collective-permute-start(bf16[16,1024]{1,0:T(8,128)(2,1)S(1)} %get-tuple-element.139), channel_id=1, source_target_pairs={{0,24},{4,28},{8,16},{12,20},{16,8},{20,12},{24,0},{28,4},{1,25},{... | collective-permute-start | bytes 98312 | tf_op jit(solution)/shard_map/ppermute | solution.py:321
  383.7 14.3 %collective-permute-start.58 = (bf16[16,1024]{1,0:T(8,128)(2,1)S(1)}, bf16[16,1024]{1,0:T(8,128)(2,1)S(1)}, u32[]{:S(2)}, u32[]{:S(2)}) collective-permute-start(bf16[16,1024]{1,0:T(8,128)(2,1)S(1)} %get-tuple-element.140), channel_id=1, source_target_pairs={{0,20},{4,16},{8,28},{12,24},{16,4},{20,0},{24,12},{28,8},{1,21},{... | collective-permute-start | bytes 98312 | tf_op jit(solution)/shard_map/ppermute | solution.py:321
  392.3 14.7 %collective-permute-start.57 = (bf16[16,1024]{1,0:T(8,128)(2,1)S(1)}, bf16[16,1024]{1,0:T(8,128)(2,1)S(1)}, u32[]{:S(2)}, u32[]{:S(2)}) collective-permute-start(bf16[16,1024]{1,0:T(8,128)(2,1)S(1)} %get-tuple-element.141), channel_id=1, source_target_pairs={{0,16},{4,20},{8,24},{12,28},{16,0},{20,4},{24,8},{28,12},{1,17},{... | collective-permute-start | bytes 98312 | tf_op jit(solution)/shard_map/ppermute | solution.py:321
  394.3 14.3 %collective-permute-start.56 = (bf16[16,1024]{1,0:T(8,128)(2,1)S(1)}, bf16[16,1024]{1,0:T(8,128)(2,1)S(1)}, u32[]{:S(2)}, u32[]{:S(2)}) collective-permute-start(bf16[16,1024]{1,0:T(8,128)(2,1)S(1)} %get-tuple-element.142), channel_id=1, source_target_pairs={{0,12},{4,8},{8,4},{12,0},{16,28},{20,24},{24,20},{28,16},{1,13},{... | collective-permute-start | bytes 98312 | tf_op jit(solution)/shard_map/ppermute | solution.py:321
  396.4 13.9 %collective-permute-start.55 = (bf16[16,1024]{1,0:T(8,128)(2,1)S(1)}, bf16[16,1024]{1,0:T(8,128)(2,1)S(1)}, u32[]{:S(2)}, u32[]{:S(2)}) collective-permute-start(bf16[16,1024]{1,0:T(8,128)(2,1)S(1)} %get-tuple-element.143), channel_id=1, source_target_pairs={{0,8},{4,12},{8,0},{12,4},{16,24},{20,28},{24,16},{28,20},{1,9},{5... | collective-permute-start | bytes 98312 | tf_op jit(solution)/shard_map/ppermute | solution.py:321
  396.6 15.9 %collective-permute-start.38 = (bf16[16,3712]{1,0:T(8,128)(2,1)S(1)}, bf16[16,3712]{1,0:T(8,128)(2,1)S(1)}, u32[]{:S(2)}, u32[]{:S(2)}) collective-permute-start(bf16[16,3712]{1,0:T(8,128)(2,1)S(1)} %get-tuple-element.123), channel_id=1, source_target_pairs={{0,4},{4,0},{8,12},{12,8},{16,20},{20,16},{24,28},{28,24},{1,5},{5... | collective-permute-start | bytes 356360 | tf_op jit(solution)/shard_map/ppermute | solution.py:321
  398.0 14.6 %collective-permute-start.44 = (bf16[16,3712]{1,0:T(8,128)(2,1)S(1)}, bf16[16,3712]{1,0:T(8,128)(2,1)S(1)}, u32[]{:S(2)}, u32[]{:S(2)}) collective-permute-start(bf16[16,3712]{1,0:T(8,128)(2,1)S(1)} %get-tuple-element.124), channel_id=1, source_target_pairs={{0,28},{4,24},{8,20},{12,16},{16,12},{20,8},{24,4},{28,0},{1,29},{... | collective-permute-start | bytes 356360 | tf_op jit(solution)/shard_map/ppermute | solution.py:321
  408.7 13.9 %collective-permute-start.42 = (bf16[16,3712]{1,0:T(8,128)(2,1)S(1)}, bf16[16,3712]{1,0:T(8,128)(2,1)S(1)}, u32[]{:S(2)}, u32[]{:S(2)}) collective-permute-start(bf16[16,3712]{1,0:T(8,128)(2,1)S(1)} %get-tuple-element.126), channel_id=1, source_target_pairs={{0,20},{4,16},{8,28},{12,24},{16,4},{20,0},{24,12},{28,8},{1,21},{... | collective-permute-start | bytes 356360 | tf_op jit(solution)/shard_map/ppermute | solution.py:321
  (67 other events, 601.2 us)
